TPU v7x, 32 devices: a whole 2x2x4 slice. The times are simulated.
32 devices in a mesh: lat: 4 (over y, x), col: 8 (over z, core).
Axes of the slice: x: 2, y: 2, z: 4, core: 2. Of those that a mesh axis runs over, the one named last changes fastest.
Arguments:
- control: float32 [128, 2048], P('lat', 'col'), may hold values from -6 to 6
- perturbations: float32 [128, 2048, 128], P('lat', 'col'), may hold values from -6 to 6
- zonal_flow: float32 [128, 2048], P('lat', 'col'), may hold values from -0.25 to 0.25
- meridional_flow: float32 [128, 2048], P('lat', 'col'), may hold values from -0.25 to 0.25
- diffusivity: float32 [128, 2048], P('lat', 'col'), may hold values from 0.03 to 0.12
- send_cell: int32 [4, 8, 8, 128], P('lat', 'col'), may hold values from 0 to 8191
- send_station: int32 [4, 8, 8, 128], P('lat', 'col'), may hold values from 0 to 255
- send_weight: float32 [4, 8, 8, 128], P('lat', 'col'), may hold values from 0.2 to 1
- send_count: int32 [4, 8, 8], P('lat', 'col'), may hold values from 32 to 128, as said below
- obs_value: float32 [2, 8192], P(None, ('lat', 'col')), may hold values from -24 to 24
- obs_error: float32 [2, 8192], P(None, ('lat', 'col')), may hold values from 1.3 to 64, as said below
Outputs:
- analysis: float32 [128, 2048, 128], P('lat', 'col')
- obs_analysis: float32 [2, 8192, 128], P(None, ('lat', 'col'))
Inputs may be any that keep to these rules, and one draw needn't show every extreme that they name: send_count[l, e, d] counts the live leading slots that device e of latitude group l fills for device d of its group; in every group one device d receives all 128 slots from every source. obs_error is positive.
All inputs are finite; a program needn't handle non-finite values.
Results may differ from a plain program's by a relative error of at most 0.0003.
Values sent between devices are 32-bit elements; how exact they have to be, the bound alone decides.
A program may use at most 128 MiB of HBM per device.

v0:
```python
import math

import jax
import jax.numpy as jnp
from jax import lax
from jax.sharding import PartitionSpec as P

exact_mode = lax.Precision.HIGHEST


def with_halo(block, sides, width):
    for axis, dim in sides:
        count = lax.axis_size(axis)
        forward = [(i, i + 1) for i in range(count - 1)]
        backward = [(target, source) for source, target in forward]
        low = lax.ppermute(
            lax.slice_in_dim(block, block.shape[dim] - width, None, axis=dim), axis, forward
        )
        high = lax.ppermute(lax.slice_in_dim(block, 0, width, axis=dim), axis, backward)
        block = jnp.concatenate([low, block, high], axis=dim)
    return block


def upwind_rates(zonal, meridional, diffusion):
    east_rate = diffusion + jnp.maximum(-zonal, 0.0)
    west_rate = diffusion + jnp.maximum(zonal, 0.0)
    north_rate = diffusion + jnp.maximum(-meridional, 0.0)
    south_rate = diffusion + jnp.maximum(meridional, 0.0)
    return (
        east_rate[..., None],
        west_rate[..., None],
        north_rate[..., None],
        south_rate[..., None],
    )


def advance(padded, coeffs):
    centre = padded[1:-1, 1:-1]
    result = centre + coeffs[0] * (padded[2:, 1:-1] - centre)
    result = result + coeffs[1] * (padded[:-2, 1:-1] - centre)
    result = result + coeffs[2] * (padded[1:-1, 2:] - centre)
    return result + coeffs[3] * (padded[1:-1, :-2] - centre)


def on_device(
    control,
    perturbations,
    zonal_flow,
    meridional_flow,
    diffusivity,
    send_cell,
    send_station,
    send_weight,
    send_count,
    obs_value,
    obs_error,
):
    members = perturbations + control[:, :, None]
    longitude_cells = perturbations.shape[2]
    owned_count = obs_value.shape[1]
    step_total = obs_value.shape[0]
    cell_ids = send_cell[0, 0]
    stations = send_station[0, 0]
    live_slot = lax.broadcasted_iota(jnp.int32, cell_ids.shape, 1) < send_count[0, 0][:, None]
    factors = jnp.where(live_slot, send_weight[0, 0], 0.0)
    station_iota = lax.broadcasted_iota(jnp.int32, (1, 1, owned_count), 2)
    arrived = lax.all_to_all(stations, "col", split_axis=0, concat_axis=0, tiled=True)
    onehot_table = (arrived[:, :, None] == station_iota).astype(jnp.float32)
    inner_rates = upwind_rates(zonal_flow, meridional_flow, diffusivity)
    prior_ensemble_matrix = []
    current_model_vector = members
    for time_index in range(step_total):
        padded = with_halo(current_model_vector, (("lat", 0), ("col", 1)), 1)
        current_model_vector = advance(padded, inner_rates)
        prior_ensemble_matrix.append(current_model_vector)
    root_scale = math.sqrt(longitude_cells - 1.0)
    gram = jnp.zeros((longitude_cells, longitude_cells), jnp.float32)
    push = jnp.zeros((longitude_cells,), jnp.float32)
    means = []
    spreads = []
    for time_index in range(step_total):
        raveled_tracer_vector = prior_ensemble_matrix[time_index].reshape(-1, longitude_cells)
        picked = raveled_tracer_vector[cell_ids.reshape(-1)].reshape(
            cell_ids.shape + (longitude_cells,)
        )
        partial_value = picked * factors[:, :, None]
        received = lax.all_to_all(partial_value, "col", split_axis=0, concat_axis=0, tiled=True)
        measurement_vector = jnp.einsum("scm,sco->om", received, onehot_table, precision=exact_mode)
        obs_mean = jnp.mean(measurement_vector, axis=1)
        spread = measurement_vector - obs_mean[:, None]
        scaled = spread / (obs_error[time_index][:, None] * root_scale)
        innovation = (obs_value[time_index] - obs_mean) / obs_error[time_index]
        gram = gram + jnp.dot(scaled.T, scaled, precision=exact_mode)
        push = push + jnp.dot(innovation, scaled, precision=exact_mode)
        means.append(obs_mean)
        spreads.append(spread)
    identity = jnp.eye(longitude_cells, dtype=jnp.float32)
    total_gram, total_push = lax.psum((gram, push), ("lat", "col"))
    factor = jnp.linalg.cholesky(identity + total_gram)
    inverse = lax.linalg.triangular_solve(factor, identity, left_side=True, lower=True)
    offset = (
        jnp.dot(inverse.T, jnp.dot(inverse, total_push, precision=exact_mode), precision=exact_mode)
        / root_scale
    )
    weights = inverse.T + offset[:, None]
    final_model_vector = prior_ensemble_matrix[-1]
    state_mean = jnp.mean(final_model_vector, axis=2, keepdims=True)
    departures = (final_model_vector - state_mean).reshape(-1, longitude_cells)
    analysis = state_mean + jnp.dot(departures, weights, precision=exact_mode).reshape(
        final_model_vector.shape
    )
    obs_analysis = jnp.stack(
        [
            means[k][:, None] + jnp.dot(spreads[k], weights, precision=exact_mode)
            for k in range(step_total)
        ]
    )
    return (analysis, obs_analysis)


def solution(mesh):
    return jax.shard_map(
        on_device,
        mesh=mesh,
        in_specs=(
            P("lat", "col"),
            P("lat", "col", None),
            P("lat", "col"),
            P("lat", "col"),
            P("lat", "col"),
            P("lat", "col", None, None),
            P("lat", "col", None, None),
            P("lat", "col", None, None),
            P("lat", "col", None),
            P(None, ("lat", "col")),
            P(None, ("lat", "col")),
        ),
        out_specs=(P("lat", "col", None), P(None, ("lat", "col"), None)),
        check_vma=False,
    )
```

profile of v0, /device:TPU:0, one launch (start us, length us, event | category | flops | bytes accessed | tf_op | source)
XLA Modules:
  0.0 279.2 jit_solution(1356697586044808981)
XLA Ops:
  7.2 6.3 %all-to-all-start = ((s32[8,1,128]{2,1,0:T(1,128)}), s32[8,1,128]{2,1,0:T(1,128)S(1)}, u32[]{:S(2)}, u32[]{:S(2)}) async-start(s32[8,1,128]{2,1,0:T(1,128)} %bitcast.76), calls=%async_computation | async-start | bytes 8192 | tf_op jit(solution)/shard_map/all_to_all | solution.py:67
  13.5 0.0 copy-start.2
  13.5 0.0 copy-start.3
  13.5 3.6 %broadcast_add_fusion = f32[32,256,128]{2,1,0:T(8,128)S(1)} fusion(f32[32,256,128]{2,1,0:T(8,128)} %param.12, f32[32,256]{1,0:T(8,128)} %param.11), kind=kLoop, calls=%fused_computation.46 | loop fusion | flops 1048576 | bytes 8421376 | tf_op jit(solution)/shard_map/add | solution.py:58
  17.2 0.0 copy-start.4
  17.2 0.0 copy-start.8
  17.2 3.4 %collective-permute-start.1 = (f32[1,256,128]{2,1,0:T(8,128)S(1)}, f32[1,256,128]{2,1,0:T(8,128)S(1)}, u32[]{:S(2)}, u32[]{:S(2)}) collective-permute-start(f32[1,256,128]{2,1,0:T(8,128)S(1)} %get-tuple-element.16), channel_id=1, source_target_pairs={{0,8},{8,16},{16,24},{1,9},{9,17},{17,25},{2,10},{10,18},{18,26},{... | collective-permute-start | bytes 393224 | tf_op jit(solution)/shard_map/ppermute | solution.py:16
  20.6 1.3 collective-permute-start
  21.9 0.0 copy-done.1
  21.9 0.0 copy-done.2
  22.0 2.0 collective-permute-done.1
  24.0 4.8 %collective-permute-done = f32[1,256,128]{2,1,0:T(8,128)S(1)} collective-permute-done((f32[1,256,128]{2,1,0:T(8,128)S(1)}, f32[1,256,128]{2,1,0:T(8,128)S(1)}, u32[]{:S(2)}, u32[]{:S(2)}) %collective-permute-start) | collective-permute-done | bytes 131104 | tf_op jit(solution)/shard_map/ppermute | solution.py:19
  28.8 1.3 collective-permute-start.2
  30.1 3.0 %collective-permute-start.3 = (f32[34,1,128]{2,1,0:T(1,128)S(1)}, f32[34,1,128]{2,1,0:T(1,128)S(1)}, u32[]{:S(2)}, u32[]{:S(2)}) collective-permute-start(f32[34,1,128]{2,1,0:T(1,128)S(1)} %get-tuple-element.13), channel_id=1, source_target_pairs={{0,1},{1,2},{2,3},{3,4},{4,5},{5,6},{6,7},{8,9},{9,10},{10,11},{11... | collective-permute-start | bytes 52232 | tf_op jit(solution)/shard_map/ppermute | solution.py:16
  33.2 0.1 bitcast_select_fusion
  33.2 0.0 collective-permute-done.2
  33.2 0.7 collective-permute-done.3
  34.0 8.6 %fusion.14 = f32[32,256,128]{2,1,0:T(8,128)S(1)} fusion(f32[32,256,128]{2,1,0:T(8,128)S(1)} %broadcast_add_fusion, f32[34,1,128]{2,1,0:T(1,128)S(1)} %collective-permute-done.3, f32[1,256,128]{2,1,0:T(8,128)S(1)} %collective-permute-done, f32[1,256,128]{2,1,0:T(8,128)S(1)} %collective-permute-done.1, f32[34,1,128]{2,1,0:T(1,128)S(1)} %collective-permute-done.2, ...), kind=kLoop, calls=%fused_computation.25 | loop fusion | flops 20971520 | bytes 8816640 | tf_op jit(solution)/shard_map/add | solution.py:42
  42.5 0.0 copy-start
  42.6 3.7 %collective-permute-start.5 = (f32[1,256,128]{2,1,0:T(8,128)S(1)}, f32[1,256,128]{2,1,0:T(8,128)S(1)}, u32[]{:S(2)}, u32[]{:S(2)}) collective-permute-start(f32[1,256,128]{2,1,0:T(8,128)S(1)} %get-tuple-element.14), channel_id=1, source_target_pairs={{0,8},{8,16},{16,24},{1,9},{9,17},{17,25},{2,10},{10,18},{18,26},{... | collective-permute-start | bytes 393224 | tf_op jit(solution)/shard_map/ppermute | solution.py:16
  46.3 1.3 collective-permute-start.4
  47.6 0.0 copy-done.5
  47.6 2.3 collective-permute-done.5
  49.9 4.6 %collective-permute-done.4 = f32[1,256,128]{2,1,0:T(8,128)S(1)} collective-permute-done((f32[1,256,128]{2,1,0:T(8,128)S(1)}, f32[1,256,128]{2,1,0:T(8,128)S(1)}, u32[]{:S(2)}, u32[]{:S(2)}) %collective-permute-start.4) | collective-permute-done | bytes 131104 | tf_op jit(solution)/shard_map/ppermute | solution.py:19
  54.5 1.3 collective-permute-start.6
  55.8 3.0 %collective-permute-start.7 = (f32[34,1,128]{2,1,0:T(1,128)S(1)}, f32[34,1,128]{2,1,0:T(1,128)S(1)}, u32[]{:S(2)}, u32[]{:S(2)}) collective-permute-start(f32[34,1,128]{2,1,0:T(1,128)S(1)} %get-tuple-element.11), channel_id=1, source_target_pairs={{0,1},{1,2},{2,3},{3,4},{4,5},{5,6},{6,7},{8,9},{9,10},{10,11},{11... | collective-permute-start | bytes 52232 | tf_op jit(solution)/shard_map/ppermute | solution.py:16
  58.8 5.0 %gather_fusion = f32[1024,128]{1,0:T(8,128)S(1)} fusion(f32[8192,128]{1,0:T(8,128)} %bitcast.68, s32[1024]{0:T(1024)S(1)} %broadcast_clamp_fusion), kind=kCustom, calls=%fused_computation | custom fusion | bytes 1052672 | tf_op jit(solution)/shard_map/gather | solution.py:83
  63.8 0.2 copy.25
  64.0 0.0 collective-permute-done.6
  64.0 0.0 collective-permute-done.7
  64.1 11.6 %fusion.51 = (f32[32,256]{1,0:T(8,128)S(1)}, f32[32,256,128]{2,1,0:T(8,128)}) fusion(f32[32,256,128]{2,1,0:T(8,128)} %copy-done, f32[1,256,128]{2,1,0:T(8,128)S(1)} %collective-permute-done.4, f32[1,256,128]{2,1,0:T(8,128)S(1)} %collective-permute-done.5, f32[34,1,128]{2,1,0:T(1,128)S(1)} %collective-permute-done.7, f32[32,256]{1,0:T(8,128)S(1)} %get-tuple-element.22, ...), kind=kLoop, calls=%fused_computation.112 | loop fusion | flops 22011904 | bytes 8849408 | tf_op jit(solution)/shard_map/reduce_sum | solution.py:107
  75.7 5.0 %gather_fusion.1 = f32[1024,128]{1,0:T(8,128)S(1)} fusion(f32[8192,128]{1,0:T(8,128)} %bitcast.69, s32[1024]{0:T(1024)S(1)} %broadcast_clamp_fusion), kind=kCustom, calls=%fused_computation.1 | custom fusion | bytes 1052672 | tf_op jit(solution)/shard_map/gather | solution.py:83
  80.7 0.2 copy.26
  80.9 1.1 broadcast_multiply_fusion
  82.0 0.0 all-to-all-done
  82.0 5.2 %all-to-all-start.1 = ((f32[8,128,128]{1,2,0:T(8,128)}), f32[8,128,128]{1,2,0:T(8,128)S(1)}, u32[]{:S(2)}, u32[]{:S(2)}) async-start(f32[8,128,128]{1,2,0:T(8,128)} %get-tuple-element.25), calls=%async_computation.1 | async-start | bytes 1048576 | tf_op jit(solution)/shard_map/all_to_all | solution.py:87
  87.2 0.0 copy-done.6
  87.3 15.3 %all-to-all-done.1 = f32[8,128,128]{1,2,0:T(8,128)S(1)} async-done(((f32[8,128,128]{1,2,0:T(8,128)}), f32[8,128,128]{1,2,0:T(8,128)S(1)}, u32[]{:S(2)}, u32[]{:S(2)}) %all-to-all-start.1) | async-done | bytes 524320 | tf_op jit(solution)/shard_map/all_to_all | solution.py:87
  102.6 3.5 %all-to-all-start.2 = ((f32[8,128,128]{1,2,0:T(8,128)}), f32[8,128,128]{1,2,0:T(8,128)S(1)}, u32[]{:S(2)}, u32[]{:S(2)}) async-start(f32[8,128,128]{1,2,0:T(8,128)} %get-tuple-element.24), calls=%async_computation.2 | async-start | bytes 1048576 | tf_op jit(solution)/shard_map/all_to_all | solution.py:87
  106.1 0.0 all-reduce.2.cloned.1.call-start
  106.2 0.6 fusion.57
  106.8 0.2 convolution_bitcast_fusion.5
  107.0 0.3 fusion.46
  107.3 14.1 %all-to-all-done.2 = f32[8,128,128]{1,2,0:T(8,128)S(1)} async-done(((f32[8,128,128]{1,2,0:T(8,128)}), f32[8,128,128]{1,2,0:T(8,128)S(1)}, u32[]{:S(2)}, u32[]{:S(2)}) %all-to-all-start.2) | async-done | bytes 524320 | tf_op jit(solution)/shard_map/all_to_all | solution.py:87
  121.4 0.6 fusion.58
  122.0 0.9 convolution_add_fusion.2
  122.9 0.0 all-reduce.2.cloned.1.call-update
  122.9 0.2 fusion.33
  123.1 37.0 %psum.15 = f32[128]{0:T(128)S(1)} all-reduce(f32[128]{0:T(128)S(1)} %fusion.33), channel_id=1, replica_groups=mesh['lat'=4,'col'=8] {'lat','col'}, use_global_device_ids=true, to_apply=%region_6.7 | all-reduce | flops 128 | bytes 1024 | tf_op jit(solution)/shard_map/psum | solution.py:98
  160.1 78.4 %all-reduce.2.cloned.1.call-done = f32[128,128]{1,0:T(8,128)} async-done(((f32[128,128]{1,0:T(8,128)}), f32[128,128]{1,0:T(8,128)}) %all-reduce.2.cloned.1.call-update) | async-done | bytes 65552 | tf_op jit(solution)/shard_map/psum | solution.py:98
  238.6 0.9 convert_add_fusion
  239.4 0.1 copy.27
  239.5 0.9 fusion.43
  240.4 11.7 %cholesky.18 = f32[128,128]{1,0:T(8,128)S(1)} custom-call(f32[128,128]{1,0:T(8,128)S(1)} %fusion.43), custom_call_target="Cholesky" | custom-call | tf_op jit(solution)/shard_map/jit(cholesky)/cholesky | solution.py:99
  252.1 0.6 compare_reduce_fusion
  252.8 0.7 fusion.38
  253.4 9.8 %custom-call.6 = f32[1,128,128]{1,2,0:T(8,128)S(1)} custom-call(f32[1,128,128]{2,1,0:T(8,128)S(1)} %fusion.38), custom_call_target="InvertDiagBlocksLowerTriangular" | custom-call | tf_op jit(solution)/shard_map/triangular_solve | solution.py:100
  263.3 0.2 fusion.41
  263.5 0.2 convolution_bitcast_fusion.3
  263.7 0.2 fusion.32
  263.9 0.3 fusion.30
  264.2 0.3 fusion.31
  264.5 7.0 %fusion.26 = f32[32,256,128]{2,1,0:T(8,128)} fusion(f32[32,256,128]{2,1,0:T(8,128)} %get-tuple-element.9, f32[32,256]{1,0:T(8,128)S(1)} %broadcast_multiply_fusion.2, f32[128,128]{1,0:T(8,128)S(1)} %fusion.41, f32[128]{0:T(128)S(1)} %fusion.32), kind=kOutput, calls=%fused_computation.44 | convolution fusion | flops 1612726272 | bytes 8487424 | tf_op jit(solution)/shard_map/dot_general | solution.py:109
  271.5 0.8 copy.31
  (23 shorter events, 0.2 us)
Async XLA Ops:
  7.2 74.8 %all-to-all-start = ((s32[8,1,128]{2,1,0:T(1,128)}), s32[8,1,128]{2,1,0:T(1,128)S(1)}, u32[]{:S(2)}, u32[]{:S(2)}) async-start(s32[8,1,128]{2,1,0:T(1,128)} %bitcast.76), calls=%async_computation | async-start | bytes 8192 | tf_op jit(solution)/shard_map/all_to_all | solution.py:67
  13.5 8.4 %copy-start.1 = (f32[32,256]{1,0:T(8,128)S(1)}, f32[32,256]{1,0:T(8,128)}, u32[]{:S(2)}) copy-start(f32[32,256]{1,0:T(8,128)} %param.15) | copy-start | bytes 98308
  13.5 8.4 %copy-start.2 = (f32[32,256]{1,0:T(8,128)S(1)}, f32[32,256]{1,0:T(8,128)}, u32[]{:S(2)}) copy-start(f32[32,256]{1,0:T(8,128)} %param.13) | copy-start | bytes 98308
  13.5 8.4 %copy-start.3 = (f32[32,256]{1,0:T(8,128)S(1)}, f32[32,256]{1,0:T(8,128)}, u32[]{:S(2)}) copy-start(f32[32,256]{1,0:T(8,128)} %param.14) | copy-start | bytes 98308
  17.2 16.0 %copy-start.4 = (f32[1,1,8,128]{3,2,1,0:T(8,128)S(1)}, f32[1,1,8,128]{3,2,1,0:T(8,128)}, u32[]{:S(2)}) copy-start(f32[1,1,8,128]{3,2,1,0:T(8,128)} %param.18) | copy-start | bytes 12292
  17.2 16.0 %copy-start.8 = (s32[1,1,8]{2,1,0:T(1,128)S(1)}, s32[1,1,8]{2,1,0:T(1,128)}, u32[]{:S(2)}) copy-start(s32[1,1,8]{2,1,0:T(1,128)} %param.19) | copy-start | bytes 100
  17.2 6.8 %collective-permute-start.1 = (f32[1,256,128]{2,1,0:T(8,128)S(1)}, f32[1,256,128]{2,1,0:T(8,128)S(1)}, u32[]{:S(2)}, u32[]{:S(2)}) collective-permute-start(f32[1,256,128]{2,1,0:T(8,128)S(1)} %get-tuple-element.16), channel_id=1, source_target_pairs={{0,8},{8,16},{16,24},{1,9},{9,17},{17,25},{2,10},{10,18},{18,26},{... | collective-permute-start | bytes 393224 | tf_op jit(solution)/shard_map/ppermute | solution.py:16
  20.6 8.2 %collective-permute-start = (f32[1,256,128]{2,1,0:T(8,128)S(1)}, f32[1,256,128]{2,1,0:T(8,128)S(1)}, u32[]{:S(2)}, u32[]{:S(2)}) collective-permute-start(f32[1,256,128]{2,1,0:T(8,128)S(1)} %get-tuple-element.17), channel_id=1, source_target_pairs={{8,0},{16,8},{24,16},{9,1},{17,9},{25,17},{10,2},{18,10},{26,18},{... | collective-permute-start | bytes 393224 | tf_op jit(solution)/shard_map/ppermute | solution.py:19
  28.8 4.4 %collective-permute-start.2 = (f32[34,1,128]{2,1,0:T(1,128)S(1)}, f32[34,1,128]{2,1,0:T(1,128)S(1)}, u32[]{:S(2)}, u32[]{:S(2)}) collective-permute-start(f32[34,1,128]{2,1,0:T(1,128)S(1)} %get-tuple-element.12), channel_id=1, source_target_pairs={{1,0},{2,1},{3,2},{4,3},{5,4},{6,5},{7,6},{9,8},{10,9},{11,10},{12... | collective-permute-start | bytes 52232 | tf_op jit(solution)/shard_map/ppermute | solution.py:19
  30.1 3.9 %collective-permute-start.3 = (f32[34,1,128]{2,1,0:T(1,128)S(1)}, f32[34,1,128]{2,1,0:T(1,128)S(1)}, u32[]{:S(2)}, u32[]{:S(2)}) collective-permute-start(f32[34,1,128]{2,1,0:T(1,128)S(1)} %get-tuple-element.13), channel_id=1, source_target_pairs={{0,1},{1,2},{2,3},{3,4},{4,5},{5,6},{6,7},{8,9},{9,10},{10,11},{11... | collective-permute-start | bytes 52232 | tf_op jit(solution)/shard_map/ppermute | solution.py:16
  34.0 13.6 %copy-start.5 = (s32[1,1,8,128]{3,2,1,0:T(8,128)S(1)}, s32[1,1,8,128]{3,2,1,0:T(8,128)}, u32[]{:S(2)}) copy-start(s32[1,1,8,128]{3,2,1,0:T(8,128)} %param.16) | copy-start | bytes 12292
  42.5 11.9 %copy-start = (f32[32,256,128]{2,1,0:T(8,128)}, f32[32,256,128]{2,1,0:T(8,128)S(1)}, u32[]{:S(2)}) copy-start(f32[32,256,128]{2,1,0:T(8,128)S(1)} %fusion.14) | copy-start | bytes 12582916
  42.6 7.3 %collective-permute-start.5 = (f32[1,256,128]{2,1,0:T(8,128)S(1)}, f32[1,256,128]{2,1,0:T(8,128)S(1)}, u32[]{:S(2)}, u32[]{:S(2)}) collective-permute-start(f32[1,256,128]{2,1,0:T(8,128)S(1)} %get-tuple-element.14), channel_id=1, source_target_pairs={{0,8},{8,16},{16,24},{1,9},{9,17},{17,25},{2,10},{10,18},{18,26},{... | collective-permute-start | bytes 393224 | tf_op jit(solution)/shard_map/ppermute | solution.py:16
  46.3 8.2 %collective-permute-start.4 = (f32[1,256,128]{2,1,0:T(8,128)S(1)}, f32[1,256,128]{2,1,0:T(8,128)S(1)}, u32[]{:S(2)}, u32[]{:S(2)}) collective-permute-start(f32[1,256,128]{2,1,0:T(8,128)S(1)} %get-tuple-element.15), channel_id=1, source_target_pairs={{8,0},{16,8},{24,16},{9,1},{17,9},{25,17},{10,2},{18,10},{26,18},{... | collective-permute-start | bytes 393224 | tf_op jit(solution)/shard_map/ppermute | solution.py:19
  54.5 9.6 %collective-permute-start.6 = (f32[34,1,128]{2,1,0:T(1,128)S(1)}, f32[34,1,128]{2,1,0:T(1,128)S(1)}, u32[]{:S(2)}, u32[]{:S(2)}) collective-permute-start(f32[34,1,128]{2,1,0:T(1,128)S(1)} %get-tuple-element.10), channel_id=1, source_target_pairs={{1,0},{2,1},{3,2},{4,3},{5,4},{6,5},{7,6},{9,8},{10,9},{11,10},{12... | collective-permute-start | bytes 52232 | tf_op jit(solution)/shard_map/ppermute | solution.py:19
  55.8 8.3 %collective-permute-start.7 = (f32[34,1,128]{2,1,0:T(1,128)S(1)}, f32[34,1,128]{2,1,0:T(1,128)S(1)}, u32[]{:S(2)}, u32[]{:S(2)}) collective-permute-start(f32[34,1,128]{2,1,0:T(1,128)S(1)} %get-tuple-element.11), channel_id=1, source_target_pairs={{0,1},{1,2},{2,3},{3,4},{4,5},{5,6},{6,7},{8,9},{9,10},{10,11},{11... | collective-permute-start | bytes 52232 | tf_op jit(solution)/shard_map/ppermute | solution.py:16
  75.7 11.5 %copy-start.6 = (f32[2,256]{1,0:T(2,128)S(1)}, f32[2,256]{1,0:T(2,128)}, u32[]{:S(2)}) copy-start(f32[2,256]{1,0:T(2,128)} %param.20) | copy-start | bytes 6148
  75.7 11.6 %copy-start.7 = (f32[2,256]{1,0:T(2,128)S(1)}, f32[2,256]{1,0:T(2,128)}, u32[]{:S(2)}) copy-start(f32[2,256]{1,0:T(2,128)} %param.21) | copy-start | bytes 6148
  82.0 20.6 %all-to-all-start.1 = ((f32[8,128,128]{1,2,0:T(8,128)}), f32[8,128,128]{1,2,0:T(8,128)S(1)}, u32[]{:S(2)}, u32[]{:S(2)}) async-start(f32[8,128,128]{1,2,0:T(8,128)} %get-tuple-element.25), calls=%async_computation.1 | async-start | bytes 1048576 | tf_op jit(solution)/shard_map/all_to_all | solution.py:87
  102.6 18.8 %all-to-all-start.2 = ((f32[8,128,128]{1,2,0:T(8,128)}), f32[8,128,128]{1,2,0:T(8,128)S(1)}, u32[]{:S(2)}, u32[]{:S(2)}) async-start(f32[8,128,128]{1,2,0:T(8,128)} %get-tuple-element.24), calls=%async_computation.2 | async-start | bytes 1048576 | tf_op jit(solution)/shard_map/all_to_all | solution.py:87
  106.1 132.5 %all-reduce.2.cloned.1.call-start = ((), (), s32[]{:S(2)}) async-start(), calls=%async_computation.3 | async-start | bytes 131072 | tf_op jit(solution)/shard_map/psum | solution.py:98
Sparse Core Ops, SparseCore 0:
  123.1 115.4 all-reduce.1
where the time goes:
time: 281 us; the launch traced here: 279 us
  waiting for transfers between devices  122 us (43%)
  other arithmetic  49.6 us (18%)
  blocking collectives  37 us (13%)
  starting transfers between devices  33.4 us (12%)
  between operations  14.4 us (5%)
  local copies, waits for them, and re-layouts  11.4 us (4%)
  matrix products  11 us (4%)
    psum x1, waiting for transfers between devices, on_device(): total_gram, total_push = lax.psum((gram, push), ('lat', 'col'))  78.4 us
    psum x1, blocking collectives, on_device(): total_gram, total_push = lax.psum((gram, push), ('lat', 'col'))  37 us
    all_to_all x2, waiting for transfers between devices, on_device(): lax.all_to_all(partial_value, 'col', split_axis=0, concat_axis=0, tiled=T...  29.4 us
    ppermute x4, starting transfers between devices, with_halo(): lax.ppermute(lax.slice_in_dim(block, block.shape[dim] - width, None, axis...  13.1 us
    another operation x3, other arithmetic, on_device(): factor = jnp.linalg.cholesky(identity + total_gram)  12.4 us
    reduce_sum x1, other arithmetic, on_device(): state_mean = jnp.mean(final_model_vector, axis=2, keepdims=True)  11.6 us
    another operation x2, other arithmetic, on_device(): lax.linalg.triangular_solve(factor, identity, left_side=True, lower=True)  10.5 us
    gather x2, local copies, waits for them, and re-layouts, on_device(): raveled_tracer_vector[cell_ids.reshape(-1)]  10 us
  transfers between devices with their start and end apart: 12, of which 8 were waited for; matrix products, arithmetic and copies ran while one was open for 13% of the time, Pallas kernels for 0%

commit v1 on v0

v1 whole, which is shorter than its diff:
```python
import functools
import math

import jax
import jax.numpy as jnp
from jax import lax
from jax.experimental import pallas as pl
from jax.experimental.pallas import tpu as pltpu
from jax.sharding import PartitionSpec as P

MESH = pl.DeviceIdType.MESH
exact_mode = lax.Precision.HIGHEST
PAD = 8


def slice_rows(members, count):
    return -(-(members + 1) // (8 * count)) * 8


def forecast_kernel(
    n_lat,
    n_col,
    control,
    perturbations,
    zonal,
    meridional,
    diffusion,
    cell,
    station,
    weight,
    live,
    obs_value,
    obs_error,
    final_out,
    observed_out,
    total_out,
    state_0,
    state_1,
    state_2,
    rates,
    columns,
    edge_send,
    edge_recv,
    side_recv,
    slots_send,
    slots_recv,
    part,
    part_recv,
    lat_part,
    total,
    load_sem,
    store_sem,
    halo_send_sem,
    halo_recv_sem,
    slots_send_sem,
    slots_recv_sem,
    part_send_sem,
    part_recv_sem,
    lat_send_sem,
    lat_recv_sem,
    total_send_sem,
    total_recv_sem,
):
    lat, col = lax.axis_index("lat"), lax.axis_index("col")
    nx, ny = control.shape
    m = perturbations.shape[2]
    cap = cell.shape[1]
    steps, owned = obs_value.shape
    states = (state_0, state_1, state_2)

    chunk = nx // 4
    loads = [
        pltpu.make_async_copy(
            perturbations.at[pl.ds(q * chunk, chunk)],
            state_0.at[pl.ds(1 + q * chunk, chunk), pl.ds(PAD, ny)],
            load_sem.at[q],
        )
        for q in range(4)
    ]
    for q in (0, 3, 1, 2):
        loads[q].start()

    barrier = pltpu.get_barrier_semaphore()

    def greet_col(o, carry):
        pl.semaphore_signal(barrier, inc=1, device_id=(lat, lax.rem(col + o, n_col)), device_id_type=MESH)
        return carry

    def greet_lat(o, carry):
        pl.semaphore_signal(barrier, inc=1, device_id=(lax.rem(lat + o, n_lat), col), device_id_type=MESH)
        return carry

    lax.fori_loop(1, n_col, greet_col, 0)
    lax.fori_loop(1, n_lat, greet_lat, 0)

    u, v, d = zonal[...], meridional[...], diffusion[...]
    fields = [
        d + jnp.maximum(-u, 0.0),
        d + jnp.maximum(u, 0.0),
        d + jnp.maximum(-v, 0.0),
        d + jnp.maximum(v, 0.0),
    ]
    rates[...] = jnp.transpose(jnp.concatenate(fields, axis=0))
    rest = jnp.zeros((128 - nx - 2 * steps, ny), jnp.float32)
    columns[...] = jnp.transpose(jnp.concatenate([control[...], obs_value[...], obs_error[...], rest], axis=0))

    def edges(t, i, low, high):
        edge_send[t, 0, pl.ds(i, 1), :] = low
        edge_send[t, 1, pl.ds(i, 1), :] = high

    def add_row(i, carry):
        shift = lax.rem(128 - i, 128)
        for j in range(0, ny, 64):
            centre = pltpu.roll(columns[j : j + 64, :], shift, 1)[:, 0:1]
            value = state_0[1 + i, PAD + j : PAD + j + 64, :] + centre
            state_0[1 + i, PAD + j : PAD + j + 64, :] = value
            if j == 0:
                edge_send[0, 0, pl.ds(i, 1), :] = value[0:1]
            if j == ny - 64:
                edge_send[0, 1, pl.ds(i, 1), :] = value[63:64]
        return carry

    def halo(t, side):
        source = states[t]
        if side == 0:
            src, dst, to = source.at[1, pl.ds(PAD, ny)], side_recv.at[t, 1], (lat - 1, col)
        elif side == 1:
            src, dst, to = source.at[nx, pl.ds(PAD, ny)], side_recv.at[t, 0], (lat + 1, col)
        elif side == 2:
            src, dst, to = edge_send.at[t, 0], edge_recv.at[t, 1], (lat, col - 1)
        else:
            src, dst, to = edge_send.at[t, 1], edge_recv.at[t, 0], (lat, col + 1)
        arrives = side ^ 1
        send = pltpu.make_async_remote_copy(
            src_ref=src,
            dst_ref=dst,
            send_sem=halo_send_sem.at[t, side],
            recv_sem=halo_recv_sem.at[t, arrives],
            device_id=to,
            device_id_type=MESH,
        )
        return send

    exists = (lat > 0, lat < n_lat - 1, col > 0, col < n_col - 1)

    def send_halo(t, side):
        @pl.when(exists[side])
        def _():
            halo(t, side).start()

    def take_halo(t, side):
        target = states[t]

        @pl.when(exists[side])
        def _():
            halo(t, side ^ 1).wait_recv()
            if side < 2:
                target[(nx + 1) * side, PAD : PAD + ny, :] = side_recv[t, side]
            else:
                at = PAD - 1 if side == 2 else PAD + ny

                def put(i, carry):
                    target[1 + i, at : at + 1, :] = edge_recv[t, side - 2, pl.ds(i, 1), :]
                    return carry

                lax.fori_loop(0, nx, put, 0)

        @pl.when(jnp.logical_not(exists[side]))
        def _():
            if side < 2:
                target[(nx + 1) * side, PAD : PAD + ny, :] = jnp.zeros((ny, m), jnp.float32)
            else:
                at = PAD - 1 if side == 2 else PAD + ny

                def put(i, carry):
                    target[1 + i, at : at + 1, :] = jnp.zeros((1, m), jnp.float32)
                    return carry

                lax.fori_loop(0, nx, put, 0)

    def step_row(t, i, carry):
        source, target = states[t], states[t + 1]
        shift = lax.rem(128 - i, 128)
        for j in range(0, ny, 64):
            k = pltpu.roll(rates[j : j + 64, :], shift, 1)
            at = PAD + j
            centre = source[1 + i, at : at + 64, :]
            value = centre + k[:, 0:1] * (source[2 + i, at : at + 64, :] - centre)
            value = value + k[:, nx : nx + 1] * (source[i, at : at + 64, :] - centre)
            value = value + k[:, 2 * nx : 2 * nx + 1] * (source[1 + i, at + 1 : at + 65, :] - centre)
            value = value + k[:, 3 * nx : 3 * nx + 1] * (source[1 + i, at - 1 : at + 63, :] - centre)
            target[1 + i, at : at + 64, :] = value
            if t + 1 < steps:
                if j == 0:
                    edge_send[t + 1, 0, pl.ds(i, 1), :] = value[0:1]
                if j == ny - 64:
                    edge_send[t + 1, 1, pl.ds(i, 1), :] = value[63:64]
        return carry

    def slot_copy(t, o):
        rows = cap + 8 if t == 0 else cap
        return pltpu.make_async_remote_copy(
            src_ref=slots_send.at[t, o, pl.ds(0, rows)],
            dst_ref=slots_recv.at[t, o, pl.ds(0, rows)],
            send_sem=slots_send_sem.at[t, o],
            recv_sem=slots_recv_sem.at[t, o],
            device_id=(lat, lax.rem(col + o, n_col)),
            device_id_type=MESH,
        )

    bits = ny.bit_length() - 1

    def fill(t, o):
        source = states[t + 1]
        receiver = lax.rem(col + o, n_col)

        def group(g, carry):
            for r in range(16):
                c = cell[receiver, g * 16 + r]
                i, j = lax.shift_right_logical(c, bits), c & (ny - 1)
                slots_send[t, o, pl.ds(g * 16 + r, 1), :] = source[1 + i, pl.ds(PAD + j, 1), :]
            return carry

        lax.fori_loop(0, cap // 16, group, 0)
        if t == 0:
            lane = lax.broadcasted_iota(jnp.int32, (1, cap), 1)
            factor = jnp.where(lane < live[0, receiver], weight[pl.ds(receiver, 1), :], 0.0)
            line = lax.broadcasted_iota(jnp.int32, (8, cap), 0)
            head = jnp.where(line == 0, station[pl.ds(receiver, 1), :].astype(jnp.float32), factor)
            slots_send[t, o, pl.ds(cap, 8), :] = head

    def nth(k):
        half = lax.div(k + 1, 2)
        return n_col // 2 + jnp.where(lax.rem(k, 2) == 1, -half, half)

    def send_slots(t):
        def one(k, carry):
            o = nth(k)
            fill(t, o)
            slot_copy(t, o).start()
            return carry

        lax.fori_loop(0, n_col - 1, one, 0)
        fill(t, 0)

    loads[0].wait()
    loads[3].wait()
    add_row(0, 0)
    add_row(nx - 1, 0)
    pl.semaphore_wait(barrier, n_col + n_lat - 2)
    send_halo(0, 0)
    send_halo(0, 1)
    loads[1].wait()
    loads[2].wait()
    lax.fori_loop(1, nx - 1, add_row, 0)
    send_halo(0, 2)
    send_halo(0, 3)

    for t in range(steps):
        take_halo(t, 2)
        take_halo(t, 3)
        lax.fori_loop(1, nx - 1, functools.partial(step_row, t), 0)
        take_halo(t, 0)
        take_halo(t, 1)
        step_row(t, 0, 0)
        step_row(t, nx - 1, 0)
        if t + 1 < steps:
            for side in range(4):
                send_halo(t + 1, side)
        send_slots(t)
    store = pltpu.make_async_copy(state_2.at[pl.ds(1, nx), pl.ds(PAD, ny)], final_out, store_sem)
    store.start()

    root_scale = math.sqrt(m - 1.0)
    part[...] = jnp.zeros_like(part)
    gram = jnp.zeros((m, m), jnp.float32)
    push = jnp.zeros((1, m), jnp.float32)
    for t in range(steps):
        line = lax.broadcasted_iota(jnp.int32, (owned, cap), 0).astype(jnp.float32)

        def product(head, values):
            mix = jnp.where(line == head[0:1], head[1:2], 0.0)
            return jnp.dot(mix, values, precision=exact_mode, preferred_element_type=jnp.float32)

        observed_out[t] = product(slots_send[0, 0, pl.ds(cap, 8), :], slots_send[t, 0, pl.ds(0, cap), :])

        def one(k, carry):
            o = nth(n_col - 2 - k)
            slot_copy(t, o).wait_recv()
            observed_out[t] += product(slots_recv[0, o, pl.ds(cap, 8), :], slots_recv[t, o, pl.ds(0, cap), :])
            return carry

        lax.fori_loop(0, n_col - 1, one, 0)
        observed = observed_out[t]
        mean = jnp.mean(observed, axis=1, keepdims=True)
        spread = observed - mean
        error = columns[:, nx + steps + t : nx + steps + t + 1]
        scaled = spread / (error * root_scale)
        innovation = (columns[:, nx + t : nx + t + 1] - mean) / error
        gram = gram + lax.dot_general(
            scaled, scaled, (((0,), (0,)), ((), ())), precision=exact_mode, preferred_element_type=jnp.float32
        )
        push = push + jnp.sum(scaled * innovation, axis=0, keepdims=True)
    part[0:m, :] = gram
    part[m : m + 1, :] = push

    rows = part_recv.shape[1]

    def mine(ref, who):
        return ref.at[pl.ds(pl.multiple_of(who * rows, 8), rows)]

    def part_copy(o):
        who = lax.rem(col + o, n_col)
        return pltpu.make_async_remote_copy(
            src_ref=mine(part, who),
            dst_ref=part_recv.at[o],
            send_sem=part_send_sem.at[o],
            recv_sem=part_recv_sem.at[o],
            device_id=(lat, who),
            device_id_type=MESH,
        )

    def lat_copy(o):
        return pltpu.make_async_remote_copy(
            src_ref=lat_part.at[0],
            dst_ref=lat_part.at[o],
            send_sem=lat_send_sem.at[o],
            recv_sem=lat_recv_sem.at[o],
            device_id=(lax.rem(lat + o, n_lat), col),
            device_id_type=MESH,
        )

    def total_copy(o, owner):
        return pltpu.make_async_remote_copy(
            src_ref=mine(total, owner),
            dst_ref=mine(total, owner),
            send_sem=total_send_sem.at[o],
            recv_sem=total_recv_sem.at[o],
            device_id=(lat, lax.rem(col + o, n_col)),
            device_id_type=MESH,
        )

    def each(count, act):
        def body(o, carry):
            act(o)
            return carry

        lax.fori_loop(1, count, body, 0)

    each(n_col, lambda o: part_copy(o).start())
    here = pl.ds(pl.multiple_of(col * rows, 8), rows)

    def add_part(o, acc):
        part_copy(o).wait_recv()
        return acc + part_recv[o]

    lat_part[0] = lax.fori_loop(1, n_col, add_part, part[here, :])
    each(n_lat, lambda o: lat_copy(o).start())

    def add_lat(o, acc):
        lat_copy(o).wait_recv()
        return acc + lat_part[o]

    total[here, :] = lax.fori_loop(1, n_lat, add_lat, lat_part[0])
    each(n_col, lambda o: total_copy(o, col).start())
    each(n_col, lambda o: total_copy(o, lax.rem(col + n_col - o, n_col)).wait_recv())
    total_out[...] = total[...]

    each(n_col, lambda o: part_copy(o).wait_send())
    each(n_lat, lambda o: lat_copy(o).wait_send())
    each(n_col, lambda o: total_copy(o, col).wait_send())
    for t in range(steps):
        each(n_col, lambda o: slot_copy(t, o).wait_send())
        for side in range(4):

            @pl.when(exists[side])
            def _():
                halo(t, side).wait_send()

    store.wait()


def on_device(
    n_lat,
    n_col,
    control,
    perturbations,
    zonal_flow,
    meridional_flow,
    diffusivity,
    send_cell,
    send_station,
    send_weight,
    send_count,
    obs_value,
    obs_error,
):
    nx, ny, m = perturbations.shape
    cap = send_cell.shape[3]
    steps, owned = obs_value.shape
    rows = slice_rows(m, n_col)
    f32 = jnp.float32
    state = pltpu.VMEM((nx + 2, ny + 2 * PAD, m), f32)
    dma = pltpu.SemaphoreType.DMA
    vmem, smem, anywhere = (pl.BlockSpec(memory_space=s) for s in (pltpu.VMEM, pltpu.SMEM, pl.ANY))
    final, observed, total = pl.pallas_call(
        functools.partial(forecast_kernel, n_lat, n_col),
        out_shape=(
            jax.ShapeDtypeStruct((nx, ny, m), f32),
            jax.ShapeDtypeStruct((steps, owned, m), f32),
            jax.ShapeDtypeStruct((n_col * rows, m), f32),
        ),
        in_specs=[vmem, anywhere, vmem, vmem, vmem, smem, vmem, vmem, smem, vmem, vmem],
        out_specs=(anywhere, vmem, vmem),
        scratch_shapes=[
            state,
            state,
            state,
            pltpu.VMEM((ny, 128), f32),
            pltpu.VMEM((ny, 128), f32),
            pltpu.VMEM((steps, 2, nx, m), f32),
            pltpu.VMEM((steps, 2, nx, m), f32),
            pltpu.VMEM((steps, 2, ny, m), f32),
            pltpu.VMEM((steps, n_col, cap + 8, m), f32),
            pltpu.VMEM((steps, n_col, cap + 8, m), f32),
            pltpu.VMEM((n_col * rows, m), f32),
            pltpu.VMEM((n_col, rows, m), f32),
            pltpu.VMEM((n_lat, rows, m), f32),
            pltpu.VMEM((n_col * rows, m), f32),
            dma((4,)),
            dma,
            dma((steps, 4)),
            dma((steps, 4)),
            dma((steps, n_col)),
            dma((steps, n_col)),
            dma((n_col,)),
            dma((n_col,)),
            dma((n_lat,)),
            dma((n_lat,)),
            dma((n_col,)),
            dma((n_col,)),
        ],
        compiler_params=pltpu.CompilerParams(
            collective_id=0, has_side_effects=True, vmem_limit_bytes=48 * 1024 * 1024
        ),
    )(
        control,
        perturbations,
        zonal_flow,
        meridional_flow,
        diffusivity,
        send_cell[0, 0],
        send_station[0, 0],
        send_weight[0, 0],
        send_count[0],
        obs_value,
        obs_error,
    )
    root_scale = math.sqrt(m - 1.0)
    identity = jnp.eye(m, dtype=f32)
    push = total[m]
    factor = jnp.linalg.cholesky(identity + total[:m])
    inverse = lax.linalg.triangular_solve(factor, identity, left_side=True, lower=True)
    offset = (
        jnp.dot(inverse.T, jnp.dot(inverse, push, precision=exact_mode), precision=exact_mode) / root_scale
    )
    weights = inverse.T + offset[:, None]

    def transform(values):
        mean = jnp.mean(values, axis=-1, keepdims=True)
        return mean + jnp.dot(
            (values - mean).reshape(-1, m), weights, precision=exact_mode
        ).reshape(values.shape)

    return transform(final), transform(observed)


def solution(mesh):
    n_lat, n_col = mesh.shape["lat"], mesh.shape["col"]
    return jax.shard_map(
        functools.partial(on_device, n_lat, n_col),
        mesh=mesh,
        in_specs=(
            P("lat", "col"),
            P("lat", "col", None),
            P("lat", "col"),
            P("lat", "col"),
            P("lat", "col"),
            P("lat", "col", None, None),
            P("lat", "col", None, None),
            P("lat", "col", None, None),
            P("lat", "col", None),
            P(None, ("lat", "col")),
            P(None, ("lat", "col")),
        ),
        out_specs=(P("lat", "col", None), P(None, ("lat", "col"), None)),
        check_vma=False,
    )
```

time: 281 us -> 122 us (0.43)
  waiting for transfers between devices: 122 us -> 0 us
  Pallas kernels: 0 us -> 76.4 us
  blocking collectives: 37 us -> 0 us
  starting transfers between devices: 33.4 us -> 0 us
  other arithmetic: 49.6 us -> 26.4 us
  between operations: 14.4 us -> 0.73 us
    psum x1 -> x0, waiting for transfers between devices: 78.4 us -> none  [on_device(): total_gram, total_push = lax.psum((gram, push), ('lat', 'col'))]
    pallas_call x0 -> x1, Pallas kernels: none -> 76.4 us  [on_device(): pl.pallas_call(functools.partial(forecast_kernel, n_lat, n_col), out_shap...]
    psum x1 -> x0, blocking collectives: 37 us -> none  [on_device(): total_gram, total_push = lax.psum((gram, push), ('lat', 'col'))]
    all_to_all x3 -> x0, waiting for transfers between devices: 29.4 us -> none  [the longest x2 29.4 us: on_device(): lax.all_to_all(partial_value, 'col', split_axis=0, concat_axis=0, tiled=T...]
    ppermute x8 -> x0, starting transfers between devices: 18.3 us -> none  [the longest x4 13.1 us: with_halo(): lax.ppermute(lax.slice_in_dim(block, block.shape[dim] - width, None, axis...]
    all_to_all x3 -> x0, starting transfers between devices: 15.1 us -> none  [the longest x2 8.74 us: on_device(): lax.all_to_all(partial_value, 'col', split_axis=0, concat_axis=0, tiled=T...]
    ppermute x8 -> x0, waiting for transfers between devices: 14.4 us -> none  [the longest x4 9.35 us: with_halo(): lax.ppermute(lax.slice_in_dim(block, 0, width, axis=dim), axis, backward)]
    add x4 -> x1, other arithmetic: 13.1 us -> 0.01 us  [on_device(): factor = jnp.linalg.cholesky(identity + total[:m])]
  transfers between devices with their start and end apart: 12 -> 0, of which waited for: 8 -> 0; matrix products, arithmetic and copies ran while one was open for 13% -> 0% of each run, Pallas kernels for 0% -> 0%
where the time goes in v1:
time: 122 us; the launch traced here: 121 us
  Pallas kernels  76.4 us (63%)
  other arithmetic  26.4 us (22%)
  local copies, waits for them, and re-layouts  9.12 us (7%)
  matrix products  8.79 us (7%)
    pallas_call x1, Pallas kernels, on_device(): pl.pallas_call(functools.partial(forecast_kernel, n_lat, n_col), out_shap...  76.4 us
    another operation x3, other arithmetic, on_device(): factor = jnp.linalg.cholesky(identity + total[:m])  12.4 us
    another operation x2, other arithmetic, on_device(): lax.linalg.triangular_solve(factor, identity, left_side=True, lower=True)  10.5 us
    unnamed x22, local copies, waits for them, and re-layouts  9.03 us
    dot_general x2, matrix products, transform(): jnp.dot((values - mean).reshape(-1, m), weights, precision=exact_mode)  8.16 us
    reduce_sum x2, other arithmetic, transform(): mean = jnp.mean(values, axis=-1, keepdims=True)  3.5 us

profile of v1, /device:TPU:0, one launch (start us, length us, event | category | flops | bytes accessed | tf_op | source)
XLA Modules:
  0.0 121.5 jit_solution(6016398154178379953)
XLA Ops:
  0.6 0.0 copy-start.1
  0.6 0.7 copy-done.1
  1.4 0.0 copy-start.2
  1.4 0.8 copy-done.2
  2.2 0.0 copy-start.3
  2.2 0.8 copy-done.3
  2.9 0.0 copy-start.4
  2.9 0.8 copy-done.4
  3.7 0.0 copy-start.5
  3.7 0.7 copy-done.5
  4.4 0.0 copy-start.6
  4.4 0.7 copy-done.6
  5.0 0.0 copy-start.7
  5.0 0.7 copy-done.7
  5.7 0.0 copy-start.8
  5.7 0.7 copy-done.8
  6.4 0.0 copy-start.9
  6.4 0.7 copy-done.9
  7.1 0.0 copy-start.10
  7.1 0.7 copy-done.10
  7.8 76.4 %shard_map.122 = (f32[32,256,128]{2,1,0:T(8,128)S(1)}, f32[2,256,128]{2,1,0:T(8,128)S(1)}, f32[192,128]{1,0:T(8,128)S(1)}) custom-call(f32[32,256]{1,0:T(8,128)S(1)} %copy-done.1, f32[32,256,128]{2,1,0:T(8,128)} %perturbations.1, f32[32,256]{1,0:T(8,128)S(1)} %copy-done.2, f32[32,256]{1,0:T(8,128)S(1)} %copy-done.3, f32[32,256]{1,0:T(8,128)S(1)} %copy-done.4, ...), custom_call_target="tpu_custom_call" | custom-call | tf_op jit(solution)/shard_map/pallas_call | solution.py:406
  84.2 0.0 copy-start
  84.2 1.9 %copy-done = f32[32,256,128]{2,1,0:T(8,128)} copy-done((f32[32,256,128]{2,1,0:T(8,128)}, f32[32,256,128]{2,1,0:T(8,128)S(1)}, u32[]{:S(2)}) %copy-start) | copy-done | bytes 4194328
  86.1 0.1 copy.13
  86.3 11.7 %cholesky.18 = f32[128,128]{1,0:T(8,128)S(1)} custom-call(f32[128,128]{1,0:T(8,128)S(1)} %fusion.15), custom_call_target="Cholesky" | custom-call | tf_op jit(solution)/shard_map/jit(cholesky)/cholesky | solution.py:462
  98.0 0.6 compare_reduce_fusion
  98.6 0.7 fusion.9
  99.3 9.8 %custom-call.6 = f32[1,128,128]{1,2,0:T(8,128)S(1)} custom-call(f32[1,128,128]{2,1,0:T(8,128)S(1)} %fusion.9), custom_call_target="InvertDiagBlocksLowerTriangular" | custom-call | tf_op jit(solution)/shard_map/triangular_solve | solution.py:463
  109.1 0.2 fusion.13
  109.4 0.2 convolution_bitcast_fusion.1
  109.6 0.2 fusion.6
  109.8 0.2 reduce_sum.19
  109.9 1.1 convolution_add_fusion
  111.1 3.3 %reduce_sum.18 = f32[32,256]{1,0:T(8,128)S(1)} reduce(f32[32,256,128]{2,1,0:T(8,128)} %copy-done, f32[]{:T(128)} %constant.44.clone.1), dimensions={2}, to_apply=%region_0.1 | reduce | flops 1040384 | bytes 4227076 | tf_op jit(solution)/shard_map/reduce_sum | solution.py:470
  114.4 7.0 %fusion.2 = f32[32,256,128]{2,1,0:T(8,128)} fusion(f32[32,256,128]{2,1,0:T(8,128)} %copy-done, f32[32,256]{1,0:T(8,128)S(1)} %broadcast_multiply_fusion, f32[128,128]{1,0:T(8,128)S(1)} %fusion.13, f32[128]{0:T(128)S(1)} %fusion.6), kind=kOutput, calls=%fused_computation.2 | convolution fusion | flops 1612726272 | bytes 8487424 | tf_op jit(solution)/shard_map/dot_general | solution.py:471
  (5 shorter events, 0.1 us)
Async XLA Ops:
  0.6 0.8 copy-start.1
  1.4 0.8 copy-start.2
  2.2 0.8 copy-start.3
  2.9 0.8 copy-start.4
  3.7 0.7 copy-start.5
  4.4 0.7 copy-start.6
  5.0 0.7 copy-start.7
  5.7 0.7 copy-start.8
  6.4 0.7 copy-start.9
  7.1 0.7 copy-start.10
  84.2 1.9 %copy-start = (f32[32,256,128]{2,1,0:T(8,128)}, f32[32,256,128]{2,1,0:T(8,128)S(1)}, u32[]{:S(2)}) copy-start(f32[32,256,128]{2,1,0:T(8,128)S(1)} %get-tuple-element.5) | copy-start | bytes 12582916

commit v2 on v1

--- a/solution.py
+++ b/solution.py
@@ -20,8 +20,21 @@
 def forecast_kernel(
     n_lat,
     n_col,
+    control_in,
+    perturbations,
+    zonal_in,
+    meridional_in,
+    diffusion_in,
+    cell_in,
+    station_in,
+    weight_in,
+    live_in,
+    obs_value_in,
+    obs_error_in,
+    final_out,
+    observed_store,
+    total_out,
     control,
-    perturbations,
     zonal,
     meridional,
     diffusion,
@@ -31,9 +44,8 @@
     live,
     obs_value,
     obs_error,
-    final_out,
     observed_out,
-    total_out,
+    wide,
     state_0,
     state_1,
     state_2,
@@ -48,6 +60,7 @@
     part_recv,
     lat_part,
     total,
+    small_sem,
     load_sem,
     store_sem,
     halo_send_sem,
@@ -77,6 +90,21 @@
         )
         for q in range(4)
     ]
+    pairs = (
+        (zonal_in, zonal),
+        (meridional_in, meridional),
+        (diffusion_in, diffusion),
+        (control_in, control),
+        (obs_value_in, obs_value),
+        (obs_error_in, obs_error),
+        (cell_in, cell),
+        (live_in, live),
+        (station_in, station),
+        (weight_in, weight),
+    )
+    smalls = [pltpu.make_async_copy(a, b, small_sem.at[q]) for q, (a, b) in enumerate(pairs)]
+    for copy in smalls:
+        copy.start()
     for q in (0, 3, 1, 2):
         loads[q].start()
 
@@ -93,6 +121,8 @@
     lax.fori_loop(1, n_col, greet_col, 0)
     lax.fori_loop(1, n_lat, greet_lat, 0)
 
+    for copy in smalls:
+        copy.wait()
     u, v, d = zonal[...], meridional[...], diffusion[...]
     fields = [
         d + jnp.maximum(-u, 0.0),
@@ -104,9 +134,13 @@
     rest = jnp.zeros((128 - nx - 2 * steps, ny), jnp.float32)
     columns[...] = jnp.transpose(jnp.concatenate([control[...], obs_value[...], obs_error[...], rest], axis=0))
 
-    def edges(t, i, low, high):
-        edge_send[t, 0, pl.ds(i, 1), :] = low
-        edge_send[t, 1, pl.ds(i, 1), :] = high
+    def widen(i, carry):
+        shift = lax.rem(128 - i, 128)
+        for j in range(0, ny, 64):
+            k = pltpu.roll(rates[j : j + 64, :], shift, 1)
+            for q in range(4):
+                wide[q, i, j : j + 64, :] = jnp.broadcast_to(k[:, q * nx : q * nx + 1], (64, m))
+        return carry
 
     def add_row(i, carry):
         shift = lax.rem(128 - i, 128)
@@ -180,15 +214,14 @@
 
     def step_row(t, i, carry):
         source, target = states[t], states[t + 1]
-        shift = lax.rem(128 - i, 128)
         for j in range(0, ny, 64):
-            k = pltpu.roll(rates[j : j + 64, :], shift, 1)
+            k = [wide[q, i, j : j + 64, :] for q in range(4)]
             at = PAD + j
             centre = source[1 + i, at : at + 64, :]
-            value = centre + k[:, 0:1] * (source[2 + i, at : at + 64, :] - centre)
-            value = value + k[:, nx : nx + 1] * (source[i, at : at + 64, :] - centre)
-            value = value + k[:, 2 * nx : 2 * nx + 1] * (source[1 + i, at + 1 : at + 65, :] - centre)
-            value = value + k[:, 3 * nx : 3 * nx + 1] * (source[1 + i, at - 1 : at + 63, :] - centre)
+            value = centre + k[0] * (source[2 + i, at : at + 64, :] - centre)
+            value = value + k[1] * (source[i, at : at + 64, :] - centre)
+            value = value + k[2] * (source[1 + i, at + 1 : at + 65, :] - centre)
+            value = value + k[3] * (source[1 + i, at - 1 : at + 63, :] - centre)
             target[1 + i, at : at + 64, :] = value
             if t + 1 < steps:
                 if j == 0:
@@ -255,6 +288,7 @@
     lax.fori_loop(1, nx - 1, add_row, 0)
     send_halo(0, 2)
     send_halo(0, 3)
+    lax.fori_loop(0, nx, widen, 0)
 
     for t in range(steps):
         take_halo(t, 2)
@@ -268,7 +302,7 @@
             for side in range(4):
                 send_halo(t + 1, side)
         send_slots(t)
-    store = pltpu.make_async_copy(state_2.at[pl.ds(1, nx), pl.ds(PAD, ny)], final_out, store_sem)
+    store = pltpu.make_async_copy(state_2.at[pl.ds(1, nx), pl.ds(PAD, ny)], final_out, store_sem.at[0])
     store.start()
 
     root_scale = math.sqrt(m - 1.0)
@@ -364,7 +398,12 @@
     total[here, :] = lax.fori_loop(1, n_lat, add_lat, lat_part[0])
     each(n_col, lambda o: total_copy(o, col).start())
     each(n_col, lambda o: total_copy(o, lax.rem(col + n_col - o, n_col)).wait_recv())
-    total_out[...] = total[...]
+    stores = (
+        pltpu.make_async_copy(total, total_out, store_sem.at[1]),
+        pltpu.make_async_copy(observed_out, observed_store, store_sem.at[2]),
+    )
+    for copy in stores:
+        copy.start()
 
     each(n_col, lambda o: part_copy(o).wait_send())
     each(n_lat, lambda o: lat_copy(o).wait_send())
@@ -378,6 +417,101 @@
                 halo(t, side).wait_send()
 
     store.wait()
+    for copy in stores:
+        copy.wait()
+
+
+def split(x):
+    high = x.astype(jnp.bfloat16)
+    return high, (x - high.astype(jnp.float32)).astype(jnp.bfloat16)
+
+
+def transform_kernel(final, observed, total, final_out, observed_out, values, results, gram, square, load_sem, store_sem):
+    cells, m = final.shape
+    watched = observed.shape[0]
+    f32 = jnp.float32
+    load_gram = pltpu.make_async_copy(total, gram, load_sem.at[0])
+    load_final = pltpu.make_async_copy(final, values.at[pl.ds(0, cells)], load_sem.at[1])
+    load_observed = pltpu.make_async_copy(observed, values.at[pl.ds(cells, watched)], load_sem.at[2])
+    load_gram.start()
+    load_observed.start()
+    load_final.start()
+
+    row, lane = (lax.broadcasted_iota(jnp.int32, (m, m), axis) for axis in (0, 1))
+    identity = jnp.where(row == lane, 1.0, 0.0).astype(f32)
+    load_gram.wait()
+    square[:, 0:m] = gram[0:m, :] + identity
+    square[:, m:] = identity
+    line = lax.broadcasted_iota(jnp.int32, (8, m), 0)
+    for low in range(0, m, 8):
+        left, right = square[low : low + 8, 0:m], square[low : low + 8, m:]
+        pivots = [jnp.broadcast_to(left[:, low + k : low + k + 1], (8, m)) for k in range(8)]
+
+        def spread(x, j):
+            return jnp.broadcast_to(x[j : j + 1, :], (8, m))
+
+        for j in range(8):
+            pivot = spread(pivots[j], j)
+            root = lax.rsqrt(pivot)
+            root = root * (1.5 - 0.5 * pivot * root * root)
+            column = jnp.where(line > j, pivots[j] * root, 0.0)
+            here = line == j
+            x, y = spread(left, j) * root, spread(right, j) * root
+            left = jnp.where(here, x, left - column * x)
+            right = jnp.where(here, y, right - column * y)
+            for k in range(j + 1, 8):
+                pivots[k] = pivots[k] - column * spread(column, k)
+        square[low : low + 8, m:] = right
+        if low + 8 < m:
+            both = jnp.concatenate([left, right], axis=1)
+            a = both.astype(jnp.bfloat16).astype(f32)
+            b = (both - a).astype(jnp.bfloat16).astype(f32)
+            c = (both - a) - b
+            one = jnp.concatenate([t[:, 0:m] for t in (a, a, b, b, a, c)], axis=0)
+            two = jnp.concatenate([a, b, a, b, c, a], axis=0)
+            update = jnp.dot(
+                jnp.transpose(one).astype(jnp.bfloat16), two.astype(jnp.bfloat16), preferred_element_type=f32
+            )
+            square[low + 8 :, :] = square[low + 8 :, :] - update[low + 8 :, :]
+    inverse = square[:, m:]
+    push = gram[m : m + 1, :]
+    inner = jnp.sum(inverse * push, axis=1, keepdims=True)
+    offset = jnp.sum(inverse * inner, axis=0, keepdims=True) / math.sqrt(m - 1.0)
+    turned = inverse + offset
+    turned = turned - jnp.mean(turned, axis=1, keepdims=True) + 1.0 / m
+    high, low = split(jnp.transpose(turned))
+    line = jnp.concatenate([high, low], axis=1)
+    mix = jnp.concatenate([line, line], axis=0)
+
+    def apply(at, size):
+        high, low = split(values[pl.ds(at, size), :])
+        both = jnp.dot(jnp.concatenate([high, low], axis=1), mix, preferred_element_type=f32)
+        results[pl.ds(at, size), :] = both[:, 0:m] + both[:, m:]
+
+    tile = cells // 16
+    load_final.wait()
+    load_observed.wait()
+
+    def store(q):
+        here = pl.ds(pl.multiple_of(q * tile, 8), tile)
+        return pltpu.make_async_copy(results.at[here], final_out.at[here], store_sem.at[q])
+
+    def one_tile(q, carry):
+        apply(pl.multiple_of(q * tile, 8), tile)
+        store(q).start()
+        return carry
+
+    apply(cells, watched)
+    store_observed = pltpu.make_async_copy(results.at[pl.ds(cells, watched)], observed_out, store_sem.at[16])
+    store_observed.start()
+    lax.fori_loop(0, 16, one_tile, 0)
+    store_observed.wait()
+
+    def finish(q, carry):
+        store(q).wait()
+        return carry
+
+    lax.fori_loop(0, 16, finish, 0)
 
 
 def on_device(
@@ -402,7 +536,7 @@
     f32 = jnp.float32
     state = pltpu.VMEM((nx + 2, ny + 2 * PAD, m), f32)
     dma = pltpu.SemaphoreType.DMA
-    vmem, smem, anywhere = (pl.BlockSpec(memory_space=s) for s in (pltpu.VMEM, pltpu.SMEM, pl.ANY))
+    anywhere = pl.BlockSpec(memory_space=pl.ANY)
     final, observed, total = pl.pallas_call(
         functools.partial(forecast_kernel, n_lat, n_col),
         out_shape=(
@@ -410,9 +544,21 @@
             jax.ShapeDtypeStruct((steps, owned, m), f32),
             jax.ShapeDtypeStruct((n_col * rows, m), f32),
         ),
-        in_specs=[vmem, anywhere, vmem, vmem, vmem, smem, vmem, vmem, smem, vmem, vmem],
-        out_specs=(anywhere, vmem, vmem),
+        in_specs=[anywhere] * 11,
+        out_specs=(anywhere,) * 3,
         scratch_shapes=[
+            pltpu.VMEM((nx, ny), f32),
+            pltpu.VMEM((nx, ny), f32),
+            pltpu.VMEM((nx, ny), f32),
+            pltpu.VMEM((nx, ny), f32),
+            pltpu.SMEM((n_col, cap), jnp.int32),
+            pltpu.VMEM((n_col, cap), jnp.int32),
+            pltpu.VMEM((n_col, cap), f32),
+            pltpu.SMEM((1, n_col), jnp.int32),
+            pltpu.VMEM((steps, owned), f32),
+            pltpu.VMEM((steps, owned), f32),
+            pltpu.VMEM((steps, owned, m), f32),
+            pltpu.VMEM((4, nx, ny, m), f32),
             state,
             state,
             state,
@@ -427,8 +573,9 @@
             pltpu.VMEM((n_col, rows, m), f32),
             pltpu.VMEM((n_lat, rows, m), f32),
             pltpu.VMEM((n_col * rows, m), f32),
+            dma((10,)),
             dma((4,)),
-            dma,
+            dma((3,)),
             dma((steps, 4)),
             dma((steps, 4)),
             dma((steps, n_col)),
@@ -441,7 +588,7 @@
             dma((n_col,)),
         ],
         compiler_params=pltpu.CompilerParams(
-            collective_id=0, has_side_effects=True, vmem_limit_bytes=48 * 1024 * 1024
+            collective_id=0, has_side_effects=True, vmem_limit_bytes=56 * 1024 * 1024
         ),
     )(
         control,
@@ -456,23 +603,23 @@
         obs_value,
         obs_error,
     )
-    root_scale = math.sqrt(m - 1.0)
-    identity = jnp.eye(m, dtype=f32)
-    push = total[m]
-    factor = jnp.linalg.cholesky(identity + total[:m])
-    inverse = lax.linalg.triangular_solve(factor, identity, left_side=True, lower=True)
-    offset = (
-        jnp.dot(inverse.T, jnp.dot(inverse, push, precision=exact_mode), precision=exact_mode) / root_scale
-    )
-    weights = inverse.T + offset[:, None]
-
-    def transform(values):
-        mean = jnp.mean(values, axis=-1, keepdims=True)
-        return mean + jnp.dot(
-            (values - mean).reshape(-1, m), weights, precision=exact_mode
-        ).reshape(values.shape)
-
-    return transform(final), transform(observed)
+    cells, watched = nx * ny, steps * owned
+    analysis, obs_analysis = pl.pallas_call(
+        transform_kernel,
+        out_shape=(jax.ShapeDtypeStruct((cells, m), f32), jax.ShapeDtypeStruct((watched, m), f32)),
+        in_specs=[anywhere] * 3,
+        out_specs=(anywhere,) * 2,
+        scratch_shapes=[
+            pltpu.VMEM((cells + watched, m), f32),
+            pltpu.VMEM((cells + watched, m), f32),
+            pltpu.VMEM(total.shape, f32),
+            pltpu.VMEM((m, 2 * m), f32),
+            dma((3,)),
+            dma((17,)),
+        ],
+        compiler_params=pltpu.CompilerParams(vmem_limit_bytes=32 * 1024 * 1024),
+    )(final.reshape(cells, m), observed.reshape(watched, m), total)
+    return analysis.reshape(nx, ny, m), obs_analysis.reshape(steps, owned, m)
 
 
 def solution(mesh):

time: 122 us -> 85.7 us (0.70)
  other arithmetic: 26.4 us -> 0 us
  matrix products: 8.79 us -> 0 us
  local copies, waits for them, and re-layouts: 9.12 us -> 4.02 us
  Pallas kernels: 76.4 us -> 80.8 us
    another operation x5 -> x0, other arithmetic: 22.9 us -> none  [the longest x3 12.4 us: on_device(): factor = jnp.linalg.cholesky(identity + total[:m])]
    pallas_call x0 -> x1, Pallas kernels: none -> 12.2 us  [on_device(): pl.pallas_call(transform_kernel, out_shape=(jax.ShapeDtypeStruct((cells,...]
    dot_general x4 -> x0, matrix products: 8.54 us -> none  [the longest x2 8.16 us: transform(): jnp.dot((values - mean).reshape(-1, m), weights, precision=exact_mode)]
    pallas_call x1, Pallas kernels: 76.4 us -> 68.6 us  [on_device(): pl.pallas_call(functools.partial(forecast_kernel, n_lat, n_col), out_shap...]
    unnamed x22 -> x6, local copies, waits for them, and re-layouts: 9.03 us -> 4.02 us
    reduce_sum x2 -> x0, other arithmetic: 3.5 us -> none  [transform(): mean = jnp.mean(values, axis=-1, keepdims=True)]
where the time goes in v2:
time: 85.7 us; the launch traced here: 85.5 us
  Pallas kernels  80.8 us (94%)
  local copies, waits for them, and re-layouts  4.02 us (5%)
    pallas_call x1, Pallas kernels, on_device(): pl.pallas_call(functools.partial(forecast_kernel, n_lat, n_col), out_shap...  68.6 us
    pallas_call x1, Pallas kernels, on_device(): pl.pallas_call(transform_kernel, out_shape=(jax.ShapeDtypeStruct((cells,...  12.2 us
    unnamed x6, local copies, waits for them, and re-layouts  4.02 us

profile of v2, /device:TPU:0, one launch (start us, length us, event | category | flops | bytes accessed | tf_op | source)
XLA Modules:
  0.0 85.5 jit_solution(7587708327806358335)
XLA Ops:
  0.6 68.6 %shard_map.122 = (f32[32,256,128]{2,1,0:T(8,128)}, f32[2,256,128]{2,1,0:T(8,128)}, f32[192,128]{1,0:T(8,128)}) custom-call(f32[32,256]{1,0:T(8,128)} %control_in.1, f32[32,256,128]{2,1,0:T(8,128)} %perturbations.1, f32[32,256]{1,0:T(8,128)} %zonal_in.1, f32[32,256]{1,0:T(8,128)} %meridional_in.1, f32[32,256]{1,0:T(8,128)} %diffusion_in.1, ...), custom_call_target="tpu_custom_call" | custom-call | tf_op jit(solution)/shard_map/pallas_call | solution.py:540
  69.3 0.0 copy-start
  69.3 2.2 %copy-done = f32[32,256,128]{2,1,0:T(8,128)S(1)} copy-done((f32[32,256,128]{2,1,0:T(8,128)S(1)}, f32[32,256,128]{2,1,0:T(8,128)}, u32[]{:S(2)}) %copy-start) | copy-done | bytes 4194328
  71.5 0.0 copy-start.1
  71.5 0.9 %copy-done.1 = f32[2,256,128]{2,1,0:T(8,128)S(1)} copy-done((f32[2,256,128]{2,1,0:T(8,128)S(1)}, f32[2,256,128]{2,1,0:T(8,128)}, u32[]{:S(2)}) %copy-start.1) | copy-done | bytes 262168
  72.4 0.0 copy-start.2
  72.4 0.9 %copy-done.2 = f32[192,128]{1,0:T(8,128)S(1)} copy-done((f32[192,128]{1,0:T(8,128)S(1)}, f32[192,128]{1,0:T(8,128)}, u32[]{:S(2)}) %copy-start.2) | copy-done | bytes 98328
  73.3 12.2 %shard_map.123 = (f32[8192,128]{1,0:T(8,128)}, f32[512,128]{1,0:T(8,128)}) custom-call(f32[8192,128]{1,0:T(8,128)S(1)} %bitcast.8, f32[512,128]{1,0:T(8,128)S(1)} %bitcast.9, f32[192,128]{1,0:T(8,128)S(1)} %copy-done.2), custom_call_target="tpu_custom_call" | custom-call | tf_op jit(solution)/shard_map/pallas_call | solution.py:607
Async XLA Ops:
  69.3 2.2 %copy-start = (f32[32,256,128]{2,1,0:T(8,128)S(1)}, f32[32,256,128]{2,1,0:T(8,128)}, u32[]{:S(2)}) copy-start(f32[32,256,128]{2,1,0:T(8,128)} %get-tuple-element.7) | copy-start | bytes 12582916
  71.5 0.9 %copy-start.1 = (f32[2,256,128]{2,1,0:T(8,128)S(1)}, f32[2,256,128]{2,1,0:T(8,128)}, u32[]{:S(2)}) copy-start(f32[2,256,128]{2,1,0:T(8,128)} %get-tuple-element.8) | copy-start | bytes 786436
  72.4 0.9 %copy-start.2 = (f32[192,128]{1,0:T(8,128)S(1)}, f32[192,128]{1,0:T(8,128)}, u32[]{:S(2)}) copy-start(f32[192,128]{1,0:T(8,128)} %get-tuple-element.9.total) | copy-start | bytes 294916

commit v3 on v2

--- a/solution.py
+++ b/solution.py
@@ -56,6 +56,8 @@
     side_recv,
     slots_send,
     slots_recv,
+    table_send,
+    table_recv,
     part,
     part_recv,
     lat_part,
@@ -67,6 +69,8 @@
     halo_recv_sem,
     slots_send_sem,
     slots_recv_sem,
+    table_send_sem,
+    table_recv_sem,
     part_send_sem,
     part_recv_sem,
     lat_send_sem,
@@ -230,28 +234,45 @@
                     edge_send[t + 1, 1, pl.ds(i, 1), :] = value[63:64]
         return carry
 
-    def slot_copy(t, o):
+    half = n_col // 2
+    side_of, place = lax.div(col, half), lax.rem(col, half)
+    mirror = (1 - side_of) * half + place
+
+    def peer(k):
+        return side_of * half + lax.rem(place + k, half)
+
+    def slot_copy(t, kind, k):
         rows = cap + 8 if t == 0 else cap
         return pltpu.make_async_remote_copy(
-            src_ref=slots_send.at[t, o, pl.ds(0, rows)],
-            dst_ref=slots_recv.at[t, o, pl.ds(0, rows)],
-            send_sem=slots_send_sem.at[t, o],
-            recv_sem=slots_recv_sem.at[t, o],
-            device_id=(lat, lax.rem(col + o, n_col)),
+            src_ref=slots_send.at[t, kind, k, pl.ds(0, rows)],
+            dst_ref=slots_recv.at[t, kind, k, pl.ds(0, rows)],
+            send_sem=slots_send_sem.at[t, kind, k],
+            recv_sem=slots_recv_sem.at[t, kind, k],
+            device_id=(lat, peer(k)),
             device_id_type=MESH,
         )
 
+    def table_copy(t):
+        return pltpu.make_async_remote_copy(
+            src_ref=table_send.at[t],
+            dst_ref=table_recv.at[t],
+            send_sem=table_send_sem.at[t],
+            recv_sem=table_recv_sem.at[t],
+            device_id=(lat, mirror),
+            device_id_type=MESH,
+        )
+
     bits = ny.bit_length() - 1
 
-    def fill(t, o):
+    def fill(t, kind, k):
         source = states[t + 1]
-        receiver = lax.rem(col + o, n_col)
+        receiver = (1 - side_of if kind == 0 else side_of) * half + lax.rem(place + k, half)
 
         def group(g, carry):
             for r in range(16):
                 c = cell[receiver, g * 16 + r]
                 i, j = lax.shift_right_logical(c, bits), c & (ny - 1)
-                slots_send[t, o, pl.ds(g * 16 + r, 1), :] = source[1 + i, pl.ds(PAD + j, 1), :]
+                slots_send[t, kind, k, pl.ds(g * 16 + r, 1), :] = source[1 + i, pl.ds(PAD + j, 1), :]
             return carry
 
         lax.fori_loop(0, cap // 16, group, 0)
@@ -260,21 +281,36 @@
             factor = jnp.where(lane < live[0, receiver], weight[pl.ds(receiver, 1), :], 0.0)
             line = lax.broadcasted_iota(jnp.int32, (8, cap), 0)
             head = jnp.where(line == 0, station[pl.ds(receiver, 1), :].astype(jnp.float32), factor)
-            slots_send[t, o, pl.ds(cap, 8), :] = head
-
-    def nth(k):
-        half = lax.div(k + 1, 2)
-        return n_col // 2 + jnp.where(lax.rem(k, 2) == 1, -half, half)
-
-    def send_slots(t):
+            slots_send[t, kind, k, pl.ds(cap, 8), :] = head
+
+    def send_slots(t, kind):
         def one(k, carry):
-            o = nth(k)
-            fill(t, o)
-            slot_copy(t, o).start()
+            fill(t, kind, k)
+            slot_copy(t, kind, k).start()
             return carry
 
-        lax.fori_loop(0, n_col - 1, one, 0)
-        fill(t, 0)
+        lax.fori_loop(1, half, one, 0)
+        fill(t, kind, 0)
+
+    def gather_sum(t, kind, target):
+        line = lax.broadcasted_iota(jnp.int32, (owned, cap), 0).astype(jnp.float32)
+
+        def product(head, values):
+            mix = jnp.where(line == head[0:1], head[1:2], 0.0)
+            return jnp.dot(mix, values, precision=exact_mode, preferred_element_type=jnp.float32)
+
+        target[t] = product(slots_send[0, kind, 0, pl.ds(cap, 8), :], slots_send[t, kind, 0, pl.ds(0, cap), :])
+
+        def one(k, carry):
+            slot_copy(t, kind, k).wait_recv()
+            target[t] += product(slots_recv[0, kind, k, pl.ds(cap, 8), :], slots_recv[t, kind, k, pl.ds(0, cap), :])
+            return carry
+
+        lax.fori_loop(1, half, one, 0)
+
+    def send_table(t):
+        gather_sum(t, 0, table_send)
+        table_copy(t).start()
 
     loads[0].wait()
     loads[3].wait()
@@ -301,30 +337,24 @@
         if t + 1 < steps:
             for side in range(4):
                 send_halo(t + 1, side)
-        send_slots(t)
+        if t > 0:
+            send_table(t - 1)
+        send_slots(t, 0)
+        send_slots(t, 1)
     store = pltpu.make_async_copy(state_2.at[pl.ds(1, nx), pl.ds(PAD, ny)], final_out, store_sem.at[0])
     store.start()
+
+    send_table(steps - 1)
+    for t in range(steps):
+        gather_sum(t, 1, observed_out)
 
     root_scale = math.sqrt(m - 1.0)
     part[...] = jnp.zeros_like(part)
     gram = jnp.zeros((m, m), jnp.float32)
     push = jnp.zeros((1, m), jnp.float32)
     for t in range(steps):
-        line = lax.broadcasted_iota(jnp.int32, (owned, cap), 0).astype(jnp.float32)
-
-        def product(head, values):
-            mix = jnp.where(line == head[0:1], head[1:2], 0.0)
-            return jnp.dot(mix, values, precision=exact_mode, preferred_element_type=jnp.float32)
-
-        observed_out[t] = product(slots_send[0, 0, pl.ds(cap, 8), :], slots_send[t, 0, pl.ds(0, cap), :])
-
-        def one(k, carry):
-            o = nth(n_col - 2 - k)
-            slot_copy(t, o).wait_recv()
-            observed_out[t] += product(slots_recv[0, o, pl.ds(cap, 8), :], slots_recv[t, o, pl.ds(0, cap), :])
-            return carry
-
-        lax.fori_loop(0, n_col - 1, one, 0)
+        table_copy(t).wait_recv()
+        observed_out[t] += table_recv[t]
         observed = observed_out[t]
         mean = jnp.mean(observed, axis=1, keepdims=True)
         spread = observed - mean
@@ -409,7 +439,9 @@
     each(n_lat, lambda o: lat_copy(o).wait_send())
     each(n_col, lambda o: total_copy(o, col).wait_send())
     for t in range(steps):
-        each(n_col, lambda o: slot_copy(t, o).wait_send())
+        each(half, lambda k: slot_copy(t, 0, k).wait_send())
+        each(half, lambda k: slot_copy(t, 1, k).wait_send())
+        table_copy(t).wait_send()
         for side in range(4):
 
             @pl.when(exists[side])
@@ -567,8 +599,10 @@
             pltpu.VMEM((steps, 2, nx, m), f32),
             pltpu.VMEM((steps, 2, nx, m), f32),
             pltpu.VMEM((steps, 2, ny, m), f32),
-            pltpu.VMEM((steps, n_col, cap + 8, m), f32),
-            pltpu.VMEM((steps, n_col, cap + 8, m), f32),
+            pltpu.VMEM((steps, 2, n_col // 2, cap + 8, m), f32),
+            pltpu.VMEM((steps, 2, n_col // 2, cap + 8, m), f32),
+            pltpu.VMEM((steps, owned, m), f32),
+            pltpu.VMEM((steps, owned, m), f32),
             pltpu.VMEM((n_col * rows, m), f32),
             pltpu.VMEM((n_col, rows, m), f32),
             pltpu.VMEM((n_lat, rows, m), f32),
@@ -578,8 +612,10 @@
             dma((3,)),
             dma((steps, 4)),
             dma((steps, 4)),
-            dma((steps, n_col)),
-            dma((steps, n_col)),
+            dma((steps, 2, n_col // 2)),
+            dma((steps, 2, n_col // 2)),
+            dma((steps,)),
+            dma((steps,)),
             dma((n_col,)),
             dma((n_col,)),
             dma((n_lat,)),
@@ -617,7 +653,7 @@
             dma((3,)),
             dma((17,)),
         ],
-        compiler_params=pltpu.CompilerParams(vmem_limit_bytes=32 * 1024 * 1024),
+        compiler_params=pltpu.CompilerParams(vmem_limit_bytes=60 * 1024 * 1024),
     )(final.reshape(cells, m), observed.reshape(watched, m), total)
     return analysis.reshape(nx, ny, m), obs_analysis.reshape(steps, owned, m)
 

time: 85.7 us -> 80.7 us (0.942)
  local copies, waits for them, and re-layouts: 4.02 us -> 0 us
  Pallas kernels: 80.8 us -> 79.9 us
    unnamed x6 -> x0, local copies, waits for them, and re-layouts: 4.02 us -> none
    pallas_call x1, Pallas kernels: 68.6 us -> 67.2 us  [on_device(): pl.pallas_call(functools.partial(forecast_kernel, n_lat, n_col), out_shap...]
where the time goes in v3:
time: 80.7 us; the launch traced here: 80.6 us
  Pallas kernels  79.9 us (99%)
    pallas_call x1, Pallas kernels, on_device(): pl.pallas_call(functools.partial(forecast_kernel, n_lat, n_col), out_shap...  67.2 us
    pallas_call x1, Pallas kernels, on_device(): pl.pallas_call(transform_kernel, out_shape=(jax.ShapeDtypeStruct((cells,...  12.7 us

profile of v3, /device:TPU:0, one launch (start us, length us, event | category | flops | bytes accessed | tf_op | source)
XLA Modules:
  0.0 80.6 jit_solution(6366037739316837462)
XLA Ops:
  0.6 67.2 %shard_map.122 = (f32[32,256,128]{2,1,0:T(8,128)}, f32[2,256,128]{2,1,0:T(8,128)}, f32[192,128]{1,0:T(8,128)}) custom-call(f32[32,256]{1,0:T(8,128)} %control_in.1, f32[32,256,128]{2,1,0:T(8,128)} %perturbations.1, f32[32,256]{1,0:T(8,128)} %zonal_in.1, f32[32,256]{1,0:T(8,128)} %meridional_in.1, f32[32,256]{1,0:T(8,128)} %diffusion_in.1, ...), custom_call_target="tpu_custom_call" | custom-call | tf_op jit(solution)/shard_map/pallas_call | solution.py:572
  67.9 12.7 %shard_map.123 = (f32[8192,128]{1,0:T(8,128)}, f32[512,128]{1,0:T(8,128)}) custom-call(f32[8192,128]{1,0:T(8,128)} %bitcast.8, f32[512,128]{1,0:T(8,128)} %bitcast.9, f32[192,128]{1,0:T(8,128)} %get-tuple-element.9.total), custom_call_target="tpu_custom_call" | custom-call | tf_op jit(solution)/shard_map/pallas_call | solution.py:643

commit v4 on v3

--- a/solution.py
+++ b/solution.py
@@ -15,6 +15,13 @@
 
 def slice_rows(members, count):
     return -(-(members + 1) // (8 * count)) * 8
+
+
+def thirds(x):
+    high = x.astype(jnp.bfloat16)
+    rest = x - high.astype(jnp.float32)
+    middle = rest.astype(jnp.bfloat16)
+    return high, middle, (rest - middle.astype(jnp.float32)).astype(jnp.bfloat16)
 
 
 def forecast_kernel(
@@ -197,11 +204,13 @@
             else:
                 at = PAD - 1 if side == 2 else PAD + ny
 
-                def put(i, carry):
-                    target[1 + i, at : at + 1, :] = edge_recv[t, side - 2, pl.ds(i, 1), :]
+                def put(g, carry):
+                    taken = edge_recv[t, side - 2, pl.ds(pl.multiple_of(g * 8, 8), 8), :]
+                    for r in range(8):
+                        target[1 + g * 8 + r, at : at + 1, :] = taken[r : r + 1]
                     return carry
 
-                lax.fori_loop(0, nx, put, 0)
+                lax.fori_loop(0, nx // 8, put, 0)
 
         @pl.when(jnp.logical_not(exists[side]))
         def _():
@@ -269,10 +278,13 @@
         receiver = (1 - side_of if kind == 0 else side_of) * half + lax.rem(place + k, half)
 
         def group(g, carry):
+            taken = []
             for r in range(16):
                 c = cell[receiver, g * 16 + r]
                 i, j = lax.shift_right_logical(c, bits), c & (ny - 1)
-                slots_send[t, kind, k, pl.ds(g * 16 + r, 1), :] = source[1 + i, pl.ds(PAD + j, 1), :]
+                taken.append(source[1 + i, pl.ds(PAD + j, 1), :])
+            for r in range(16):
+                slots_send[t, kind, k, pl.ds(g * 16 + r, 1), :] = taken[r]
             return carry
 
         lax.fori_loop(0, cap // 16, group, 0)
@@ -296,8 +308,16 @@
         line = lax.broadcasted_iota(jnp.int32, (owned, cap), 0).astype(jnp.float32)
 
         def product(head, values):
-            mix = jnp.where(line == head[0:1], head[1:2], 0.0)
-            return jnp.dot(mix, values, precision=exact_mode, preferred_element_type=jnp.float32)
+            pick = jnp.where(line == head[0:1], 1.0, 0.0).astype(jnp.bfloat16)
+            high, middle, low = thirds(values * jnp.transpose(head)[:, 1:2])
+            upper = jnp.concatenate([high, low], axis=1)
+            lower = jnp.concatenate([middle, jnp.zeros_like(middle)], axis=1)
+            both = jnp.dot(
+                jnp.concatenate([pick, pick], axis=1),
+                jnp.concatenate([upper, lower], axis=0),
+                preferred_element_type=jnp.float32,
+            )
+            return both[:, :m] + both[:, m:]
 
         target[t] = product(slots_send[0, kind, 0, pl.ds(cap, 8), :], slots_send[t, kind, 0, pl.ds(0, cap), :])
 
@@ -350,7 +370,7 @@
 
     root_scale = math.sqrt(m - 1.0)
     part[...] = jnp.zeros_like(part)
-    gram = jnp.zeros((m, m), jnp.float32)
+    members = []
     push = jnp.zeros((1, m), jnp.float32)
     for t in range(steps):
         table_copy(t).wait_recv()
@@ -361,11 +381,20 @@
         error = columns[:, nx + steps + t : nx + steps + t + 1]
         scaled = spread / (error * root_scale)
         innovation = (columns[:, nx + t : nx + t + 1] - mean) / error
-        gram = gram + lax.dot_general(
-            scaled, scaled, (((0,), (0,)), ((), ())), precision=exact_mode, preferred_element_type=jnp.float32
-        )
+        members.append(scaled)
         push = push + jnp.sum(scaled * innovation, axis=0, keepdims=True)
-    part[0:m, :] = gram
+    scaled = jnp.concatenate(members, axis=0)
+    high, middle, low = thirds(scaled)
+    turned = jnp.transpose(scaled)
+    turned_high, turned_middle, _ = thirds(turned)
+    products = jnp.dot(
+        jnp.concatenate([turned_high, turned_middle], axis=0),
+        jnp.concatenate([high, middle], axis=1),
+        preferred_element_type=jnp.float32,
+    )
+    cross = jnp.dot(turned_high, low, preferred_element_type=jnp.float32)
+    small = products[m:, m:] + cross + jnp.transpose(cross)
+    part[0:m, :] = products[:m, :m] + (products[:m, m:] + products[m:, :m] + small)
     part[m : m + 1, :] = push
 
     rows = part_recv.shape[1]

time: 80.7 us -> 81.1 us (level)
  no operation moved by 1% of the time
where the time goes in v4:
time: 81.1 us; the launch traced here: 80.9 us
  Pallas kernels  80.3 us (99%)
    pallas_call x1, Pallas kernels, on_device(): pl.pallas_call(functools.partial(forecast_kernel, n_lat, n_col), out_shap...  67.6 us
    pallas_call x1, Pallas kernels, on_device(): pl.pallas_call(transform_kernel, out_shape=(jax.ShapeDtypeStruct((cells,...  12.7 us

profile of v4, /device:TPU:0, one launch (start us, length us, event | category | flops | bytes accessed | tf_op | source)
XLA Modules:
  0.0 80.9 jit_solution(4456886951129101772)
XLA Ops:
  0.6 67.6 %shard_map.122 = (f32[32,256,128]{2,1,0:T(8,128)}, f32[2,256,128]{2,1,0:T(8,128)}, f32[192,128]{1,0:T(8,128)}) custom-call(f32[32,256]{1,0:T(8,128)} %control_in.1, f32[32,256,128]{2,1,0:T(8,128)} %perturbations.1, f32[32,256]{1,0:T(8,128)} %zonal_in.1, f32[32,256]{1,0:T(8,128)} %meridional_in.1, f32[32,256]{1,0:T(8,128)} %diffusion_in.1, ...), custom_call_target="tpu_custom_call" | custom-call | tf_op jit(solution)/shard_map/pallas_call | solution.py:601
  68.2 12.7 %shard_map.123 = (f32[8192,128]{1,0:T(8,128)}, f32[512,128]{1,0:T(8,128)}) custom-call(f32[8192,128]{1,0:T(8,128)} %bitcast.8, f32[512,128]{1,0:T(8,128)} %bitcast.9, f32[192,128]{1,0:T(8,128)} %get-tuple-element.9.total), custom_call_target="tpu_custom_call" | custom-call | tf_op jit(solution)/shard_map/pallas_call | solution.py:672
